TPU v7x, 32 devices: a whole 2x2x4 slice. The times are simulated.
32 devices in a mesh: dp: 8 (over y, x, core), tensor: 4 (over z).
Axes of the slice: x: 2, y: 2, z: 4, core: 2. Of those that a mesh axis runs over, the one named last changes fastest.
Arguments:
- residual: bfloat16 [128, 7168], P('dp'), may hold values from -6 to 6
- query_latent: bfloat16 [128, 128, 512], P('dp', 'tensor'), may hold values from -64 to 64
- query_rope: bfloat16 [128, 128, 64], P('dp', 'tensor'), may hold values from -6 to 6
- cache_latent: bfloat16 [128, 1024, 512], P('dp'), may hold values from -4 to 4
- cache_rope: bfloat16 [128, 64, 1024], P('dp'), may hold values from -6 to 6
- lengths: int32 [128], P('dp'), may hold values from 256 to 1024, as said below
- value_up: bfloat16 [128, 512, 128], P('tensor'), may hold values from -0.25 to 0.25
- out_proj: bfloat16 [16384, 7168], P('tensor', 'dp'), may hold values from -0.5 to 0.5
- gate_proj: bfloat16 [8, 7168, 1024], P('dp', None, 'tensor'), may hold values from -0.0625 to 0.0625
- up_proj: bfloat16 [8, 7168, 1024], P('dp', None, 'tensor'), may hold values from -0.0625 to 0.0625
- down_proj: bfloat16 [8, 1024, 7168], P('dp', 'tensor'), may hold values from -0.1875 to 0.1875
- groups: int32 [128, 4], P('dp'), may hold values from 0 to 3, as said below
- expert_picks: int32 [128, 8], P('dp'), may hold values from 0 to 7, as said below
- gate_levels: int32 [128, 8], P('dp'), may hold values from 1 to 255
Outputs:
- layer_out: bfloat16 [128, 7168], P('dp')
Inputs may be any that keep to these rules, and one draw needn't show every extreme that they name: Row r attends to cache positions 0 to lengths[r] - 1; in every draw some row has length 1024. Each row names 4 different groups; among the rows of one index of dp no group is named by more than 16 rows. `expert_picks`: each row's 8 entries differ, so its experts differ. Among the rows of one index of dp no expert is named by more than 16 rows; in every draw one expert is named by exactly 16 rows of every index of dp.
All inputs are finite; a program needn't handle non-finite values.
Results may differ from a plain program's by a relative error of at most 0.02.
Values may be sent and summed in bfloat16 or wider, within the bound.
A program may use at most 128 MiB of HBM per device.

v0:
```python
import jax
import jax.numpy as jnp
from jax import lax
from jax.sharding import PartitionSpec as P

TOPG = 4


score_scale = 192.0 ** (-0.5)
route_scale = 2.5
far_below = -1e30


def attend_rows(query_latent, query_rope, cache_latent, cache_rope, lengths):
    positions = cache_latent.shape[1]
    latent_term = jnp.einsum(
        "bhl,bsl->bhs", query_latent, cache_latent, preferred_element_type=jnp.float32
    )
    rope_term = jnp.einsum(
        "bhi,bis->bhs", query_rope, cache_rope, preferred_element_type=jnp.float32
    )
    scores = (latent_term + rope_term) * score_scale
    visible = jnp.arange(positions)[None, None, :] < lengths[:, None, None]
    scores = jnp.where(visible, scores, far_below)
    highest = jnp.max(scores, axis=2, keepdims=True)
    raised = jnp.exp(scores - highest)
    weights = (raised / jnp.sum(raised, axis=2, keepdims=True)).astype(jnp.bfloat16)
    mixture = jnp.einsum("bhs,bsl->bhl", weights, cache_latent, preferred_element_type=jnp.float32)
    return mixture.astype(jnp.bfloat16)


def route_tables(groups, expert_picks, gate_levels, owners):
    group_count = min(8, owners // 2)
    per_group = owners // group_count
    slot_group = expert_picks // per_group
    slot_range = jnp.arange(groups.shape[1], dtype=jnp.int32)
    picked_group = jnp.sum(
        jnp.where(slot_group[:, :, None] == slot_range[None, None, :], groups[:, None, :], 0),
        axis=2,
    )
    expert_ids = picked_group * per_group + expert_picks % per_group
    levels = gate_levels.astype(jnp.float32)
    gates = route_scale * levels / jnp.sum(levels, axis=1, keepdims=True)
    expert_range = jnp.arange(owners, dtype=jnp.int32)
    matches = expert_ids[:, :, None] == expert_range[None, None, :]
    coefficients = jnp.sum(jnp.where(matches, gates[:, :, None], 0.0), axis=1)
    selected = jnp.any(matches, axis=1)
    level_for = jnp.sum(jnp.where(matches, gate_levels[:, :, None], 0), axis=1)
    return (coefficients, selected, level_for)


def slot_table(member, capacity):
    counts = member.astype(jnp.int32)
    ranking = jnp.cumsum(counts, axis=0) - counts
    placed = member[:, :, None] & (
        ranking[:, :, None] == jnp.arange(capacity, dtype=jnp.int32)[None, None, :]
    )
    return jnp.transpose(placed, (1, 2, 0)).astype(jnp.float32)


def expert_block(arrivals, gate_weight, up_weight, down_weight):
    gated = jnp.einsum("sid,df->sif", arrivals, gate_weight, preferred_element_type=jnp.float32)
    upward = jnp.einsum("sid,df->sif", arrivals, up_weight, preferred_element_type=jnp.float32)
    activation = (jax.nn.silu(gated) * upward).astype(jnp.bfloat16)
    produced = jnp.einsum(
        "sif,fd->sid", activation, down_weight, preferred_element_type=jnp.float32
    )
    return lax.psum(produced.astype(jnp.bfloat16), "tensor")


def local(
    residual,
    query_latent,
    query_rope,
    cache_latent,
    cache_rope,
    lengths,
    value_up,
    out_proj,
    gate_proj,
    up_proj,
    down_proj,
    groups,
    expert_picks,
    gate_levels,
):
    row_count, model_width = residual.shape
    owners = lax.axis_size("dp")
    group_count = min(8, owners // 2)
    capacity = min(row_count, TOPG * ((row_count + group_count - 1) // group_count))
    latent_mix = attend_rows(query_latent, query_rope, cache_latent, cache_rope, lengths)
    head_out = jnp.einsum(
        "bhl,hlv->bhv", latent_mix, value_up, preferred_element_type=jnp.float32
    ).astype(jnp.bfloat16)
    head_out = head_out.reshape(row_count, -1)
    column_terms = jnp.dot(
        lax.all_gather(head_out, "dp", axis=0, tiled=True),
        out_proj,
        preferred_element_type=jnp.float32,
    )
    summed_terms = lax.psum(column_terms, "tensor")
    attention = lax.all_to_all(
        summed_terms.astype(jnp.bfloat16), "dp", split_axis=0, concat_axis=1, tiled=True
    )
    hidden = (residual.astype(jnp.float32) + attention.astype(jnp.float32)).astype(jnp.bfloat16)
    coefficients, selected, level_for = route_tables(groups, expert_picks, gate_levels, owners)
    gate_weight = gate_proj[0]
    up_weight = up_proj[0]
    down_weight = down_proj[0]
    slot_place = slot_table(selected, capacity)
    outgoing = jnp.einsum(
        "ecr,rd->ecd", slot_place.astype(jnp.bfloat16), hidden, preferred_element_type=jnp.float32
    ).astype(jnp.bfloat16)
    produced = expert_block(
        lax.all_to_all(outgoing, "dp", split_axis=0, concat_axis=0, tiled=True),
        gate_weight,
        up_weight,
        down_weight,
    )
    returned = lax.all_to_all(produced, "dp", split_axis=0, concat_axis=0, tiled=True)
    weighting = slot_place * jnp.transpose(coefficients)[:, None, :]
    routed = jnp.einsum(
        "ecr,ecd->rd", weighting, returned.astype(jnp.float32), precision=lax.Precision.HIGHEST
    )
    return (hidden.astype(jnp.float32) + routed).astype(jnp.bfloat16)


def solution(mesh):
    return jax.shard_map(
        local,
        mesh=mesh,
        in_specs=(
            P("dp", None),
            P("dp", "tensor", None),
            P("dp", "tensor", None),
            P("dp", None, None),
            P("dp", None, None),
            P("dp"),
            P("tensor", None, None),
            P("tensor", "dp"),
            P("dp", None, "tensor"),
            P("dp", None, "tensor"),
            P("dp", "tensor", None),
            P("dp", None),
            P("dp", None),
            P("dp", None),
        ),
        out_specs=P("dp", None),
        check_vma=False,
    )
```

profile of v0, /device:TPU:0, one launch (start us, length us, event | category | flops | bytes accessed | tf_op | source)
XLA Modules:
  0.0 260.8 jit_solution(11801705341347301772)
XLA Ops:
  6.5 0.0 copy-start
  6.5 0.0 all-gather.2.cloned.1.call-start
  6.5 0.9 iota_compare_fusion.1
  7.4 0.7 copy-done
  8.1 0.0 copy-start.4
  8.1 2.7 %fusion.43 = f32[16,32,1024]{2,1,0:T(8,128)} fusion(bf16[16,32,64]{2,1,0:T(8,128)(2,1)} %param.16, bf16[16,64,1024]{2,1,0:T(8,128)(2,1)S(1)} %copy-done), kind=kOutput, calls=%fused_computation.63 | convolution fusion | flops 67108864 | bytes 4259840 | tf_op jit(solution)/shard_map/bhi,bis->bhs/dot_general | solution.py:19
  10.9 0.0 copy-done.4
  10.9 12.7 %multiply_select_fusion = f32[16,32,1024]{2,1,0:T(8,128)} fusion(f32[16,32,1024]{2,1,0:T(8,128)} %fusion.43, bf16[16,32,512]{2,1,0:T(8,128)(2,1)S(1)} %copy-done.4, bf16[16,1024,512]{2,1,0:T(8,128)(2,1)} %param.17, pred[16,1024]{1,0:T(8,128)(4,1)S(1)} %iota_compare_fusion.1), kind=kOutput, calls=%fused_computation.13 | convolution fusion | flops 538443776 | bytes 21512192 | tf_op jit(solution)/shard_map/bhl,bsl->bhs/dot_general | solution.py:16
  23.6 2.7 %fusion.42 = f32[16,32]{1,0:T(8,128)S(1)} fusion(f32[16,32,1024]{2,1,0:T(8,128)} %multiply_select_fusion), kind=kOutput, calls=%fused_computation.62 | output fusion | flops 1049599 | bytes 2099200 | tf_op jit(solution)/shard_map/sub | solution.py:26
  26.3 10.1 %convolution_convert_fusion.2 = bf16[16,32,512]{2,1,0:T(8,128)(2,1)S(1)} fusion(bf16[16,1024,512]{2,1,0:T(8,128)(2,1)} %param.17, f32[16,32]{1,0:T(8,128)S(1)} %fusion.42, f32[16,32,1024]{2,1,0:T(8,128)} %multiply_select_fusion), kind=kOutput, calls=%fused_computation.14 | convolution fusion | flops 538707456 | bytes 19400704 | tf_op jit(solution)/shard_map/bhs,bsl->bhl/dot_general | solution.py:28
  36.3 0.0 copy-start.5
  36.3 0.0 copy-start.7
  36.3 3.1 %fusion.8 = bf16[32,2,8,128]{3,2,1,0:T(8,128)(2,1)S(1)} fusion(bf16[32,512,128]{2,1,0:T(8,128)(2,1)} %param.20, bf16[16,32,512]{2,1,0:T(8,128)(2,1)S(1)} %convolution_convert_fusion.2), kind=kOutput, calls=%fused_computation.16 | convolution fusion | flops 67174400 | bytes 4849664 | tf_op jit(solution)/shard_map/bhl,hlv->bhv/dot_general | solution.py:92
  39.4 0.7 copy.47
  40.1 0.0 all-gather.2.cloned.1.call-update
  40.1 0.0 copy-done.5
  40.1 0.0 copy-done.7
  40.2 0.1 copy.35
  40.3 0.1 copy.37
  40.4 26.1 %all-gather.2.cloned.1.call-done = bf16[128,4096]{1,0:T(8,128)(2,1)} async-done(((bf16[16,4096]{1,0:T(8,128)(2,1)}), bf16[128,4096]{1,0:T(8,128)(2,1)}) %all-gather.2.cloned.1.call-update) | async-done | bytes 1048592 | tf_op jit(solution)/shard_map/all_gather | solution.py:97
  66.4 4.7 %fusion.44 = f32[128,896]{1,0:T(8,128)S(1)} fusion(bf16[128,4096]{1,0:T(8,128)(2,1)} %all-gather.2.cloned.1.call-done, bf16[4096,896]{1,0:T(8,128)(2,1)} %param.21), kind=kOutput, calls=%fused_computation.64 | convolution fusion | flops 939524096 | bytes 8847360 | tf_op jit(solution)/shard_map/dot_general | solution.py:96
  71.1 0.0 copy-start.3
  71.1 29.6 %all-reduce.4 = bf16[128,896]{1,0:T(8,128)(2,1)} all-reduce(f32[128,896]{1,0:T(8,128)S(1)} %fusion.44), channel_id=1, replica_groups=mesh['dp'=8,'tensor'=4] {'tensor'}, use_global_device_ids=true, to_apply=%region_2.3 | all-reduce | flops 114688 | bytes 688128 | tf_op jit(solution)/shard_map/psum | solution.py:101
  100.8 3.4 %all-to-all-start = ((bf16[8,16,896]{2,1,0:T(8,128)(2,1)}), bf16[8,16,896]{2,1,0:T(8,128)(2,1)S(1)}, u32[]{:S(2)}, u32[]{:S(2)}) async-start(bf16[8,16,896]{2,1,0:T(8,128)(2,1)} %bitcast.1), calls=%async_computation | async-start | bytes 458752 | tf_op jit(solution)/shard_map/all_to_all | solution.py:102
  104.2 0.0 all-reduce.3.cloned.1.call-start
  104.2 0.1 copy.38
  104.3 6.4 %all-to-all-done = bf16[8,16,896]{2,1,0:T(8,128)(2,1)S(1)} async-done(((bf16[8,16,896]{2,1,0:T(8,128)(2,1)}), bf16[8,16,896]{2,1,0:T(8,128)(2,1)S(1)}, u32[]{:S(2)}, u32[]{:S(2)}) %all-to-all-start) | async-done | bytes 229408 | tf_op jit(solution)/shard_map/all_to_all | solution.py:102
  110.8 0.0 copy-done.3
  110.8 0.7 convolution_convert_fusion.1
  111.5 0.0 copy-start.2
  111.5 26.5 %all_to_all.23 = bf16[8,16,7168]{2,1,0:T(8,128)(2,1)S(1)} all-to-all(bf16[8,16,7168]{2,1,0:T(8,128)(2,1)S(1)} %convolution_convert_fusion.1), channel_id=1, replica_groups=mesh['dp'=8,'tensor'=4] {'dp'}, dimensions={0} | all-to-all | bytes 3670016 | tf_op jit(solution)/shard_map/all_to_all | solution.py:115
  138.0 0.0 copy-start.1
  138.0 1.3 copy-done.1
  139.3 0.0 copy-done.2
  139.3 0.6 fusion.6
  139.9 7.1 %convolution_convert_fusion = bf16[8,16,7168]{2,1,0:T(8,128)(2,1)} fusion(bf16[1,256,7168]{2,1,0:T(8,128)(2,1)} %param.24, bf16[8,16,7168]{2,1,0:T(8,128)(2,1)} %copy-done.1, bf16[1,7168,256]{2,1,0:T(8,128)(2,1)} %param.23, f32[8,16,256]{2,1,0:T(8,128)S(1)} %fusion.6), kind=kOutput, calls=%fused_computation.1 | convolution fusion | flops 940638208 | bytes 11141120 | tf_op jit(solution)/shard_map/sif,fd->sid/dot_general | solution.py:65
  147.0 0.0 all-reduce.3.cloned.1.call-update
  147.0 0.0 copy-start.6
  147.0 74.4 %all-reduce.3.cloned.1.call-done = bf16[8,16,7168]{2,1,0:T(8,128)(2,1)} async-done(((bf16[8,16,7168]{2,1,0:T(8,128)(2,1)}), bf16[8,16,7168]{2,1,0:T(8,128)(2,1)}) %all-reduce.3.cloned.1.call-update) | async-done | bytes 1835024 | tf_op jit(solution)/shard_map/psum | solution.py:68
  221.5 4.3 %all-to-all-start.2 = ((bf16[8,16,7168]{2,1,0:T(8,128)(2,1)}), bf16[8,16,7168]{2,1,0:T(8,128)(2,1)}, u32[]{:S(2)}, u32[]{:S(2)}) async-start(bf16[8,16,7168]{2,1,0:T(8,128)(2,1)} %all-reduce.3.cloned.1.call-done), calls=%async_computation.2 | async-start | bytes 3670016 | tf_op jit(solution)/shard_map/all_to_all | solution.py:120
  225.8 0.0 copy-done.6
  225.9 23.8 %all-to-all-done.2 = bf16[8,16,7168]{2,1,0:T(8,128)(2,1)} async-done(((bf16[8,16,7168]{2,1,0:T(8,128)(2,1)}), bf16[8,16,7168]{2,1,0:T(8,128)(2,1)}, u32[]{:S(2)}, u32[]{:S(2)}) %all-to-all-start.2) | async-done | bytes 1835040 | tf_op jit(solution)/shard_map/all_to_all | solution.py:120
  249.6 4.3 %fusion.2 = bf16[16,7168]{1,0:T(8,128)(2,1)} fusion(bf16[8,16,7168]{2,1,0:T(8,128)(2,1)} %all-to-all-done.2, f32[8,16]{1,0:T(8,128)S(1)} %bitcast.62, s32[8,16]{1,0:T(8,128)S(1)} %copy.38, pred[8,16]{1,0:T(8,128)(4,1)S(1)} %bitcast.61, f32[16,7168]{1,0:T(8,128)S(1)} %bitcast.58, bf16[16,7168]{1,0:T(8,128)(2,1)S(1)} %copy-done.3), kind=kOutput, calls=%fused_computation.5 | convolution fusion | flops 176855040 | bytes 2753664 | tf_op jit(solution)/shard_map/ecr,ecd->rd/dot_general | solution.py:122
  (12 shorter events, 0.2 us)
Async XLA Ops:
  6.5 1.6 copy-start
  6.5 59.9 %all-gather.2.cloned.1.call-start = ((), (), s32[]{:S(2)}) async-start(), calls=%async_computation.3 | async-start | bytes 1179648 | tf_op jit(solution)/shard_map/all_gather | solution.py:97
  8.1 2.7 %copy-start.4 = (bf16[16,32,512]{2,1,0:T(8,128)(2,1)S(1)}, bf16[16,32,512]{2,1,0:T(8,128)(2,1)}, u32[]{:S(2)}) copy-start(bf16[16,32,512]{2,1,0:T(8,128)(2,1)} %param.15) | copy-start | bytes 1572868
  36.3 3.8 %copy-start.5 = (s32[16,8]{0,1:T(8,128)S(1)}, s32[16,8]{0,1:T(8,128)}, u32[]{:S(2)}) copy-start(s32[16,8]{0,1:T(8,128)} %param.26) | copy-start | bytes 1540
  36.3 3.8 %copy-start.7 = (s32[16,4]{0,1:T(4,128)S(1)}, s32[16,4]{0,1:T(4,128)}, u32[]{:S(2)}) copy-start(s32[16,4]{0,1:T(4,128)} %param.25) | copy-start | bytes 772
  71.1 39.7 %copy-start.3 = (bf16[16,7168]{1,0:T(8,128)(2,1)S(1)}, bf16[16,7168]{1,0:T(8,128)(2,1)}, u32[]{:S(2)}) copy-start(bf16[16,7168]{1,0:T(8,128)(2,1)} %param.14) | copy-start | bytes 688132
  100.8 9.9 %all-to-all-start = ((bf16[8,16,896]{2,1,0:T(8,128)(2,1)}), bf16[8,16,896]{2,1,0:T(8,128)(2,1)S(1)}, u32[]{:S(2)}, u32[]{:S(2)}) async-start(bf16[8,16,896]{2,1,0:T(8,128)(2,1)} %bitcast.1), calls=%async_computation | async-start | bytes 458752 | tf_op jit(solution)/shard_map/all_to_all | solution.py:102
  104.2 117.3 %all-reduce.3.cloned.1.call-start = ((), (), s32[]{:S(2)}) async-start(), calls=%async_computation.4 | async-start | bytes 3670016 | tf_op jit(solution)/shard_map/psum | solution.py:68
  111.5 27.8 %copy-start.2 = (bf16[1,7168,256]{2,1,0:T(8,128)(2,1)S(1)}, bf16[1,7168,256]{2,1,0:T(8,128)(2,1)}, u32[]{:S(2)}) copy-start(bf16[1,7168,256]{2,1,0:T(8,128)(2,1)} %param.22) | copy-start | bytes 11010052
  138.0 1.3 copy-start.1
  147.0 78.8 %copy-start.6 = (s32[16,8]{0,1:T(8,128)S(1)}, s32[16,8]{0,1:T(8,128)}, u32[]{:S(2)}) copy-start(s32[16,8]{0,1:T(8,128)} %param.27) | copy-start | bytes 1540
  221.5 28.2 %all-to-all-start.2 = ((bf16[8,16,7168]{2,1,0:T(8,128)(2,1)}), bf16[8,16,7168]{2,1,0:T(8,128)(2,1)}, u32[]{:S(2)}, u32[]{:S(2)}) async-start(bf16[8,16,7168]{2,1,0:T(8,128)(2,1)} %all-reduce.3.cloned.1.call-done), calls=%async_computation.2 | async-start | bytes 3670016 | tf_op jit(solution)/shard_map/all_to_all | solution.py:120
Sparse Core Ops, SparseCore 0:
  40.2 26.1 all-gather.1
  147.1 74.2 all-reduce.2
where the time goes:
time: 261 us
  waiting for transfers between devices  131 us (50%)
  blocking collectives  56.1 us (21%)
  matrix products  45.9 us (18%)
  between operations  13.6 us (5%)
  starting transfers between devices  7.77 us (3%)
  other arithmetic  3.72 us (1%)
  local copies, waits for them, and re-layouts  2.94 us (1%)
    psum x1, waiting for transfers between devices, expert_block(): return lax.psum(produced.astype(jnp.bfloat16), 'tensor')  74.4 us
    psum x1, blocking collectives, local(): summed_terms = lax.psum(column_terms, 'tensor')  29.6 us
    all_to_all x1, blocking collectives, local(): lax.all_to_all(outgoing, 'dp', split_axis=0, concat_axis=0, tiled=True)  26.5 us
    all_gather x1, waiting for transfers between devices, local(): lax.all_gather(head_out, 'dp', axis=0, tiled=True)  26.1 us
    all_to_all x1, waiting for transfers between devices, local(): lax.all_to_all(produced, 'dp', split_axis=0, concat_axis=0, tiled=True)  23.8 us
    dot_general x1, matrix products, attend_rows(): jnp.einsum('bhl,bsl->bhs', query_latent, cache_latent, preferred_element_...  12.7 us
    dot_general x1, matrix products, attend_rows(): jnp.einsum('bhs,bsl->bhl', weights, cache_latent, preferred_element_type=...  10.1 us
    dot_general x1, matrix products, expert_block(): jnp.einsum('sif,fd->sid', activation, down_weight, preferred_element_type...  7.07 us
  transfers between devices with their start and end apart: 4, of which 4 were waited for; matrix products, arithmetic and copies ran while one was open for 0% of the time, Pallas kernels for 0%

commit v1 on v0

v1 whole, which is shorter than its diff:
```python
import functools

import jax
import jax.numpy as jnp
from jax import lax
from jax.experimental import pallas as pl
from jax.experimental.pallas import tpu as pltpu
from jax.sharding import PartitionSpec as P

score_scale = 192.0 ** (-0.5)
route_scale = 2.5
far_below = -1e30
MIB = 1 << 20
F32 = jnp.float32
BF16 = jnp.bfloat16


def attend_kernel(
    step_rows, owners, per_group, lengths, q_lat, q_rope, c_lat, c_rope, resid, groups, picks,
    levels, value_up, head_ref, resid_ref, coef_ref, mix_s, value_s, value_sem,
):
    step = pl.program_id(0)
    rows = resid.shape[0]
    heads = q_lat.shape[1]
    positions = c_lat.shape[1]
    width = value_up.shape[2]
    fetch = pltpu.make_async_copy(value_up, value_s, value_sem)

    @pl.when(step == 0)
    def _first():
        fetch.start()
        cols = resid_ref.shape[2]
        for j in range(owners):
            resid_ref[j] = resid[:, j * cols : (j + 1) * cols]
        lane = lax.broadcasted_iota(jnp.int32, coef_ref.shape, 1)
        level = levels[...].astype(F32)
        gates = route_scale * level / jnp.sum(level, axis=1, keepdims=True)
        group = groups[...]
        pick_all = picks[...]
        total = jnp.zeros(coef_ref.shape, F32)
        for k in range(pick_all.shape[1]):
            pick = pick_all[:, k : k + 1]
            expert = pick
            for s in range(group.shape[1]):
                inside = (pick >= s * per_group) & (pick < (s + 1) * per_group)
                shifted = pick + (group[:, s : s + 1] - s) * per_group
                expert = jnp.where(inside, shifted, expert)
            total += jnp.where(lane == expert, gates[:, k : k + 1], 0.0)
        coef_ref[...] = total

    for i in range(step_rows):
        row = step * step_rows + i
        scores = lax.dot_general(
            q_lat[i], c_lat[i], (((1,), (1,)), ((), ())), preferred_element_type=F32
        )
        scores += jnp.dot(q_rope[i], c_rope[i], preferred_element_type=F32)
        place = lax.broadcasted_iota(jnp.int32, (heads, positions), 1)
        scores = jnp.where(place < lengths[row], scores * score_scale, far_below)
        highest = jnp.max(scores, axis=1, keepdims=True)
        raised = jnp.exp(scores - highest)
        total = jnp.sum(raised, axis=1, keepdims=True)
        weights = (raised / total).astype(BF16)
        mix_s[row] = jnp.dot(weights, c_lat[i], preferred_element_type=F32)

    @pl.when(step == pl.num_programs(0) - 1)
    def _last():
        fetch.wait()
        for h in range(heads):
            mixed = mix_s[:, h, :].astype(BF16)
            head = jnp.dot(mixed, value_s[h], preferred_element_type=F32)
            head_ref[:, h * width : (h + 1) * width] = head.astype(BF16)


def attend(owners, per_group, residual, query_latent, query_rope, cache_latent, cache_rope,
           lengths, value_up, groups, expert_picks, gate_levels):
    rows, heads, lat = query_latent.shape
    positions = cache_latent.shape[1]
    rope = query_rope.shape[2]
    width = value_up.shape[2]
    model = residual.shape[1]
    step_rows = 2
    whole = lambda shape: pl.BlockSpec(shape, lambda i: (0,) * len(shape))
    per_step = lambda a, b: pl.BlockSpec((step_rows, a, b), lambda i: (i, 0, 0))
    return pl.pallas_call(
        functools.partial(attend_kernel, step_rows, owners, per_group),
        grid=(rows // step_rows,),
        in_specs=[
            pl.BlockSpec(memory_space=pltpu.SMEM),
            per_step(heads, lat),
            per_step(heads, rope),
            per_step(positions, lat),
            per_step(rope, positions),
            whole(residual.shape),
            whole(groups.shape),
            whole(expert_picks.shape),
            whole(gate_levels.shape),
            pl.BlockSpec(memory_space=pl.ANY),
        ],
        out_specs=[
            whole((rows, heads * width)),
            whole((owners, rows, model // owners)),
            whole((rows, 128)),
        ],
        out_shape=[
            jax.ShapeDtypeStruct((rows, heads * width), BF16),
            jax.ShapeDtypeStruct((owners, rows, model // owners), BF16),
            jax.ShapeDtypeStruct((rows, 128), F32),
        ],
        scratch_shapes=[
            pltpu.VMEM((rows, heads, lat), F32),
            pltpu.VMEM(value_up.shape, BF16),
            pltpu.SemaphoreType.DMA,
        ],
        compiler_params=pltpu.CompilerParams(vmem_limit_bytes=32 * MIB),
        cost_estimate=pl.CostEstimate(
            flops=rows * heads * positions * 1088 * 2, bytes_accessed=24 * MIB, transcendentals=0
        ),
    )(lengths, query_latent, query_rope, cache_latent, cache_rope, residual, groups,
      expert_picks, gate_levels, value_up)


def flip(index, mask, size):
    out, bit = 0, 1
    while bit < size:
        here = index // bit % 2
        out = out + bit * ((here + 1) % 2 if mask & bit else here)
        bit *= 2
    return out


def layer_kernel(
    dp, tp, head, resid, coef, wo_h, wg_h, wu_h, wd_h, hid_out, routed_out,
    wo, wg, wu, wd, hbuf, cbuf, resb, acc, pbuf, rbuf, hid, accg, accu, pd, sr, xs, xr, zs, zr, fin,
    w_sem, c_s, c_r, a_s, a_r, f_s, f_r, q_s, q_r, b_s, b_r, z_s, z_r, x_s, x_r, y_s, y_r,
    d_s, d_r, e_s, e_r, g_s, g_r, o_s, o_r,
):
    d = lax.axis_index("dp")
    t = lax.axis_index("tensor")
    chips = dp // 2
    chip, core = d // 2, d % 2
    sib = chip * 2 + (1 - core)
    row_n = head.shape[0]
    rows = dp * row_n
    quarter = rows // tp
    cols = wo.shape[1]
    depth = wo.shape[0]
    part = fin.shape[2]
    per_quarter = dp // tp
    far_first = list(range(chips - 1, 0, -1))

    def send(src, dst, ss, rs, **where):
        copy = pltpu.make_async_remote_copy(
            src_ref=src, dst_ref=dst, send_sem=ss, recv_sem=rs,
            device_id=where, device_id_type=pl.DeviceIdType.MESH,
        )
        return copy

    loads = [
        pltpu.make_async_copy(src, dst, w_sem.at[i])
        for i, (src, dst) in enumerate(((wo_h, wo), (wg_h.at[0], wg), (wu_h.at[0], wu), (wd_h.at[0], wd)))
    ]
    for load in loads:
        load.start()

    barrier = pltpu.get_barrier_semaphore()
    for k in range(1, dp):
        pl.semaphore_signal(barrier, inc=1, device_id={"dp": (d + k) % dp}, device_id_type=pl.DeviceIdType.MESH)
    for k in range(1, tp):
        pl.semaphore_signal(barrier, inc=1, device_id={"tensor": (t + k) % tp}, device_id_type=pl.DeviceIdType.MESH)
    pl.semaphore_wait(barrier, dp - 1 + tp - 1)

    pending = []

    gather = {}
    for j in far_first:
        gather[j] = send(head, hbuf.at[d], a_s.at[j], a_r.at[j], dp=flip(chip, j, chips) * 2 + core)
        gather[j].start()
    gather[0] = send(head, hbuf.at[d], a_s.at[0], a_r.at[0], dp=sib)
    gather[0].start()
    pending += gather.values()
    hbuf[d] = head[...]

    coefs = []
    for k in range(1, dp):
        coefs.append(send(coef, cbuf.at[d], c_s.at[k], c_r.at[k], dp=(d + k) % dp))
        coefs[-1].start()
    pending += coefs
    cbuf[d] = coef[...]

    mine = d // per_quarter == t
    slot = d % per_quarter
    shares = [
        send(resid.at[(d + k) % dp], resb.at[slot], q_s.at[k], q_r.at[slot], dp=(d + k) % dp)
        for k in range(1, dp)
    ]

    @pl.when(mine)
    def _share():
        for copy in shares:
            copy.start()
        resb[slot] = resid[d]

    forwards = []
    for j in range(1, chips):
        gather[j].wait_recv()
        block = flip(chip, j, chips) * 2 + core
        forwards.append(send(hbuf.at[block], hbuf.at[block], f_s.at[j], f_r.at[j], dp=sib))
        forwards[-1].start()
    pending += forwards
    loads[0].wait()
    gather[0].wait_recv()
    for copy in forwards:
        copy.wait_recv()

    acc[...] = jnp.zeros_like(acc)
    chunk = 512

    @pl.loop(0, depth // chunk)
    def _project(k):
        at = pl.ds(pl.multiple_of(k * chunk, chunk), chunk)
        acc[...] += jnp.dot(
            hbuf[:, :, at].reshape(rows, chunk), wo[at, :], preferred_element_type=F32
        )

    for u in range(tp):
        pbuf[u] = acc[u * quarter : (u + 1) * quarter, :].astype(BF16)
    sums = []
    for k in range(1, tp):
        u = (t + k) % tp
        sums.append(send(pbuf.at[u], rbuf.at[k - 1], b_s.at[k], b_r.at[k], tensor=u))
        sums[-1].start()
    pending += sums
    for i in range(per_quarter):
        owner = t * per_quarter + i

        @pl.when(owner != d)
        def _arrive():
            send(resid.at[0], resb.at[i], q_s.at[0], q_r.at[i], dp=owner).wait_recv()

    my_rows = pl.ds(pl.multiple_of(t * quarter, quarter), quarter)
    piece = acc[my_rows, :]
    for k in range(1, tp):
        sums[k - 1].wait_recv()
        piece += rbuf[k - 1].astype(F32)
    attention = piece.astype(BF16).astype(F32)
    hid[d, my_rows, :] = (attention + resb[...].reshape(quarter, cols).astype(F32)).astype(BF16)

    along = []
    for k in range(1, tp):
        along.append(send(hid.at[d, my_rows], hid.at[d, my_rows], z_s.at[k], z_r.at[k], tensor=(t + k) % tp))
        along[-1].start()
    pending += along
    spread = {}
    for k in range(tp):
        if k:
            along[k - 1].wait_recv()
        at = pl.ds(pl.multiple_of((t + tp - k) % tp * quarter, quarter), quarter)
        for j in far_first:
            spread[k, j] = send(hid.at[d, at], hid.at[d, at], x_s.at[k, j], x_r.at[k, j], dp=flip(chip, j, chips) * 2 + core)
            spread[k, j].start()
        spread[k, 0] = send(hid.at[d, at], hid.at[d, at], x_s.at[k, 0], x_r.at[k, 0], dp=sib)
        spread[k, 0].start()
    pending += spread.values()

    loads[1].wait()
    loads[2].wait()
    accg[...] = jnp.zeros_like(accg)
    accu[...] = jnp.zeros_like(accu)

    def expand(block):
        at = pl.ds(pl.multiple_of(block * cols, cols), cols)
        values = hid[block]
        accg[...] += jnp.dot(values, wg[at, :], preferred_element_type=F32)
        accu[...] += jnp.dot(values, wu[at, :], preferred_element_type=F32)

    expand(d)
    passed = {}
    for k in range(tp):
        at = pl.ds(pl.multiple_of((t + tp - k) % tp * quarter, quarter), quarter)
        for j in range(1, chips):
            spread[k, j].wait_recv()
            block = flip(chip, j, chips) * 2 + core
            passed[k, j] = send(hid.at[block, at], hid.at[block, at], y_s.at[k, j], y_r.at[k, j], dp=sib)
            passed[k, j].start()
    pending += passed.values()
    for k in range(tp):
        spread[k, 0].wait_recv()

    @pl.loop(0, chips - 1)
    def _same(j):
        expand((chip + 1 + j) % chips * 2 + core)

    expand(sib)
    for copy in passed.values():
        copy.wait_recv()

    @pl.loop(0, chips - 1)
    def _other(j):
        expand((chip + 1 + j) % chips * 2 + 1 - core)

    for copy in coefs:
        copy.wait_recv()
    table = cbuf[...].reshape(rows, 128)
    lane = lax.broadcasted_iota(jnp.int32, (rows, 128), 1)
    weight = jnp.sum(jnp.where(lane == d, table, 0.0), axis=1, keepdims=True)
    gated = accg[...]
    active = (gated / (1.0 + jnp.exp(-gated)) * accu[...] * weight).astype(BF16)

    loads[3].wait()
    order = [(t + k) % tp for k in list(range(1, tp)) + [0]]
    halves = []
    for n, c in enumerate(order):
        at = pl.ds(pl.multiple_of(c * part, part), part)
        produced = jnp.dot(active, wd[:, at], preferred_element_type=F32).astype(BF16)
        for b in range(dp):
            pd[n, b % 2, b // 2] = produced[b * row_n : (b + 1) * row_n, :]
        halves.append(send(pd.at[n, 1 - core], sr.at[n], d_s.at[n], d_r.at[n], dp=sib))
        halves[-1].start()
    pending += halves
    across = {}
    for n in range(tp):
        halves[n].wait_recv()
        xs[n] = (pd[n, core].astype(F32) + sr[n].astype(F32)).astype(BF16)
        for j in far_first:
            peer = flip(chip, j, chips)
            across[n, j] = send(xs.at[n, peer], xr.at[n, j - 1], e_s.at[n, j], e_r.at[n, j], dp=peer * 2 + core)
            across[n, j].start()
    pending += across.values()
    reduced = []
    for n in range(tp):
        total = xs[n, chip].astype(F32)
        for j in range(1, chips):
            across[n, j].wait_recv()
            total += xr[n, j - 1].astype(F32)
        if n < tp - 1:
            zs[n] = total.astype(BF16)
            reduced.append(send(zs.at[n], zr.at[n], g_s.at[n], g_r.at[n], tensor=order[n]))
            reduced[-1].start()
    pending += reduced
    for n in range(tp - 1):
        reduced[n].wait_recv()
        total += zr[n].astype(F32)
    fin[t] = total.astype(BF16)
    last = []
    for k in range(1, tp):
        last.append(send(fin.at[t], fin.at[t], o_s.at[k], o_r.at[k], tensor=(t + k) % tp))
        last[-1].start()
    pending += last
    hid_out[...] = hid[:, pl.ds(pl.multiple_of(d * row_n, row_n), row_n), :]
    for copy in last:
        copy.wait_recv()
    routed_out[...] = fin[...]
    for copy in pending:
        copy.wait_send()

    @pl.when(mine)
    def _shared():
        for copy in shares:
            copy.wait_send()


def layer(dp, tp, head, resid, coef, wo, wg, wu, wd):
    row_n = head.shape[0]
    rows = dp * row_n
    depth, cols = wo.shape
    model, units = wg.shape[1:]
    quarter = rows // tp
    part = model // tp
    chips = dp // 2
    vm = lambda *shape: pltpu.VMEM(shape, BF16)
    sem = lambda *shape: pltpu.SemaphoreType.DMA(shape)
    return pl.pallas_call(
        functools.partial(layer_kernel, dp, tp),
        out_shape=[
            jax.ShapeDtypeStruct((dp, row_n, cols), BF16),
            jax.ShapeDtypeStruct((tp, row_n, part), BF16),
        ],
        in_specs=[pl.BlockSpec(memory_space=pltpu.VMEM)] * 3 + [pl.BlockSpec(memory_space=pl.ANY)] * 4,
        out_specs=[pl.BlockSpec(memory_space=pltpu.VMEM)] * 2,
        scratch_shapes=[
            vm(depth, cols), vm(model, units), vm(model, units), vm(units, model),
            vm(dp, row_n, depth), pltpu.VMEM((dp, row_n, 128), F32), vm(dp // tp, row_n, cols),
            pltpu.VMEM((rows, cols), F32), vm(tp, quarter, cols), vm(tp - 1, quarter, cols),
            vm(dp, rows, cols), pltpu.VMEM((rows, units), F32), pltpu.VMEM((rows, units), F32),
            vm(tp, 2, chips, row_n, part), vm(tp, chips, row_n, part), vm(tp, chips, row_n, part),
            vm(tp, chips - 1, row_n, part), vm(tp - 1, row_n, part), vm(tp - 1, row_n, part),
            vm(tp, row_n, part),
            sem(4), sem(dp), sem(dp), sem(chips), sem(chips), sem(chips), sem(chips),
            sem(dp), sem(dp // tp), sem(tp), sem(tp), sem(tp), sem(tp),
            sem(tp, chips), sem(tp, chips), sem(tp, chips), sem(tp, chips),
            sem(tp), sem(tp), sem(tp, chips), sem(tp, chips), sem(tp), sem(tp), sem(tp), sem(tp),
        ],
        compiler_params=pltpu.CompilerParams(
            collective_id=0, has_side_effects=True, vmem_limit_bytes=56 * MIB
        ),
        cost_estimate=pl.CostEstimate(
            flops=2 * rows * (depth * cols + 3 * model * units),
            bytes_accessed=20 * MIB, transcendentals=0,
        ),
    )(head, resid, coef, wo, wg, wu, wd)


def local(
    dp, tp, residual, query_latent, query_rope, cache_latent, cache_rope, lengths, value_up, out_proj,
    gate_proj, up_proj, down_proj, groups, expert_picks, gate_levels,
):
    rows, model = residual.shape
    per_group = dp // min(8, dp // 2)
    head, resid, coef = attend(
        dp, per_group, residual, query_latent, query_rope, cache_latent, cache_rope, lengths,
        value_up, groups, expert_picks, gate_levels,
    )
    hidden, routed = layer(dp, tp, head, resid, coef, out_proj, gate_proj, up_proj, down_proj)
    hidden = jnp.transpose(hidden, (1, 0, 2)).reshape(rows, model)
    routed = jnp.transpose(routed, (1, 0, 2)).reshape(rows, model)
    return (hidden.astype(F32) + routed.astype(F32)).astype(BF16)


def solution(mesh):
    return jax.shard_map(
        functools.partial(local, mesh.shape["dp"], mesh.shape["tensor"]),
        mesh=mesh,
        in_specs=(
            P("dp", None),
            P("dp", "tensor", None),
            P("dp", "tensor", None),
            P("dp", None, None),
            P("dp", None, None),
            P("dp"),
            P("tensor", None, None),
            P("tensor", "dp"),
            P("dp", None, "tensor"),
            P("dp", None, "tensor"),
            P("dp", "tensor", None),
            P("dp", None),
            P("dp", None),
            P("dp", None),
        ),
        out_specs=P("dp", None),
        check_vma=False,
    )
```

time: 261 us -> 94.7 us (0.36)
  waiting for transfers between devices: 131 us -> 0 us
  Pallas kernels: 0 us -> 80 us
  blocking collectives: 56.1 us -> 0 us
  matrix products: 45.9 us -> 0 us
  between operations: 13.6 us -> 0.06 us
  local copies, waits for them, and re-layouts: 2.94 us -> 11.6 us
  starting transfers between devices: 7.77 us -> 0 us
    pallas_call x0 -> x2, Pallas kernels: none -> 80 us  [the longest x1 63.4 us: layer(): pl.pallas_call(functools.partial(layer_kernel, dp, tp), out_shape=[jax.Sh...]
    psum x1 -> x0, waiting for transfers between devices: 74.4 us -> none  [expert_block(): return lax.psum(produced.astype(jnp.bfloat16), 'tensor')]
    dot_general x9 -> x0, matrix products: 45.9 us -> none  [the longest x1 12.7 us: attend_rows(): jnp.einsum('bhl,bsl->bhs', query_latent, cache_latent, preferred_element_...]
    all_to_all x2 -> x0, waiting for transfers between devices: 30.2 us -> none  [the longest x1 23.8 us: local(): lax.all_to_all(produced, 'dp', split_axis=0, concat_axis=0, tiled=True)]
    psum x1 -> x0, blocking collectives: 29.6 us -> none  [local(): summed_terms = lax.psum(column_terms, 'tensor')]
    all_to_all x1 -> x0, blocking collectives: 26.5 us -> none  [local(): lax.all_to_all(outgoing, 'dp', split_axis=0, concat_axis=0, tiled=True)]
    all_gather x1 -> x0, waiting for transfers between devices: 26.1 us -> none  [local(): lax.all_gather(head_out, 'dp', axis=0, tiled=True)]
    unnamed x16 -> x21, local copies, waits for them, and re-layouts: 2.01 us -> 11.5 us
  transfers between devices with their start and end apart: 4 -> 0, of which waited for: 4 -> 0; matrix products, arithmetic and copies ran while one was open for 0% -> 0% of each run, Pallas kernels for 0% -> 0%
where the time goes in v1:
time: 94.7 us; the launch traced here: 94.3 us
  Pallas kernels  80 us (84%)
  local copies, waits for them, and re-layouts  11.6 us (12%)
  other arithmetic  2.67 us (3%)
    pallas_call x1, Pallas kernels, layer(): pl.pallas_call(functools.partial(layer_kernel, dp, tp), out_shape=[jax.Sh...  63.4 us
    pallas_call x1, Pallas kernels, attend(): pl.pallas_call(functools.partial(attend_kernel, step_rows, owners, per_gr...  16.5 us
    unnamed x21, local copies, waits for them, and re-layouts  11.5 us
    unnamed x2, other arithmetic  1.94 us

profile of v1, /device:TPU:0, one launch (start us, length us, event | category | flops | bytes accessed | tf_op | source)
XLA Modules:
  0.0 94.3 jit_solution(17893707672528923301)
XLA Ops:
  0.0 0.8 copy.18.groups
  0.8 0.8 copy.19.picks
  1.5 0.8 copy.20.levels
  2.3 0.0 copy-start
  2.3 2.2 %copy-done = bf16[32,512,128]{2,1,0:T(8,128)(2,1)S(1)} copy-done((bf16[32,512,128]{2,1,0:T(8,128)(2,1)S(1)}, bf16[32,512,128]{2,1,0:T(8,128)(2,1)}, u32[]{:S(2)}) %copy-start) | copy-done | bytes 4194328
  4.5 0.0 copy-start.1
  4.5 1.6 %copy-done.1 = bf16[16,64,1024]{2,1,0:T(8,128)(2,1)S(1)} copy-done((bf16[16,64,1024]{2,1,0:T(8,128)(2,1)S(1)}, bf16[16,64,1024]{2,1,0:T(8,128)(2,1)}, u32[]{:S(2)}) %copy-start.1) | copy-done | bytes 2097176
  6.1 0.0 copy-start.2
  6.1 1.0 %copy-done.2 = bf16[16,32,512]{2,1,0:T(8,128)(2,1)S(1)} copy-done((bf16[16,32,512]{2,1,0:T(8,128)(2,1)S(1)}, bf16[16,32,512]{2,1,0:T(8,128)(2,1)}, u32[]{:S(2)}) %copy-start.2) | copy-done | bytes 524312
  7.1 0.0 copy-start.3
  7.1 0.9 copy-done.3
  8.0 0.0 copy-start.5
  8.0 0.9 copy-done.5
  8.9 0.0 copy-start.8
  8.9 0.7 copy-done.8
  9.6 16.5 %shard_map.136 = (bf16[16,4096]{1,0:T(8,128)(2,1)S(1)}, bf16[8,16,896]{2,1,0:T(8,128)(2,1)S(1)}, f32[16,128]{1,0:T(8,128)S(1)}) custom-call(s32[16]{0:T(128)S(1)} %copy-done.8, bf16[16,32,512]{2,1,0:T(8,128)(2,1)S(1)} %copy-done.2, bf16[16,32,64]{2,1,0:T(8,128)(2,1)S(1)} %copy-done.5, bf16[16,1024,512]{2,1,0:T(8,128)(2,1)} %c_lat.1, ...), custom_call_target="tpu_custom_call" | custom-call | flops 1140850688 | bytes 25165824 | tf_op jit(solution)/shard_map/pallas_call | solution.py:84
  26.1 0.0 copy-start.4
  26.1 0.7 copy-done.4
  26.8 0.0 copy-start.6
  26.8 0.6 copy-done.6
  27.5 0.0 copy-start.7
  27.5 0.6 copy-done.7
  28.1 63.4 %shard_map.137 = (bf16[8,16,896]{2,1,0:T(8,128)(2,1)}, bf16[4,16,1792]{2,1,0:T(8,128)(2,1)}) custom-call(bf16[16,4096]{1,0:T(8,128)(2,1)} %copy-done.6, bf16[8,16,896]{2,1,0:T(8,128)(2,1)} %copy-done.4, f32[16,128]{1,0:T(8,128)} %copy-done.7, bf16[4096,896]{1,0:T(8,128)(2,1)} %wo_h.1, bf16[1,7168,256]{2,1,0:T(8,128)(2,1)} %wg_h.1, ...), custom_call_target="tpu_custom_call" | custom-call | flops 2348810240 | bytes 20971520 | tf_op jit(solution)/shard_map/pallas_call | solution.py:372
  91.5 1.0 %convert_bitcast_fusion.1 = f32[8,2,8,896]{3,2,1,0:T(8,128)S(1)} fusion(bf16[8,16,896]{2,1,0:T(8,128)(2,1)} %get-tuple-element.13), kind=kLoop, calls=%fused_computation.1 | loop fusion | flops 114688 | bytes 688128
  92.5 1.0 %convert_bitcast_fusion = f32[4,2,8,1792]{3,2,1,0:T(8,128)S(1)} fusion(bf16[4,16,1792]{2,1,0:T(8,128)(2,1)} %get-tuple-element.14), kind=kLoop, calls=%fused_computation | loop fusion | flops 114688 | bytes 688128
  93.5 0.7 add_convert_fusion
  (2 shorter events, 0.1 us)
Async XLA Ops:
  2.3 2.2 %copy-start = (bf16[32,512,128]{2,1,0:T(8,128)(2,1)S(1)}, bf16[32,512,128]{2,1,0:T(8,128)(2,1)}, u32[]{:S(2)}) copy-start(bf16[32,512,128]{2,1,0:T(8,128)(2,1)} %value_up.1) | copy-start | bytes 12582916
  4.5 1.6 %copy-start.1 = (bf16[16,64,1024]{2,1,0:T(8,128)(2,1)S(1)}, bf16[16,64,1024]{2,1,0:T(8,128)(2,1)}, u32[]{:S(2)}) copy-start(bf16[16,64,1024]{2,1,0:T(8,128)(2,1)} %c_rope.1) | copy-start | bytes 6291460
  6.1 1.0 %copy-start.2 = (bf16[16,32,512]{2,1,0:T(8,128)(2,1)S(1)}, bf16[16,32,512]{2,1,0:T(8,128)(2,1)}, u32[]{:S(2)}) copy-start(bf16[16,32,512]{2,1,0:T(8,128)(2,1)} %q_lat.1) | copy-start | bytes 1572868
  7.1 0.9 copy-start.3
  8.0 0.9 copy-start.5
  8.9 0.7 copy-start.8
  26.1 0.7 copy-start.4
  26.8 0.6 copy-start.6
  27.5 0.6 copy-start.7

commit v2 on v1

v2 whole, which is shorter than its diff:
```python
import functools

import jax
import jax.numpy as jnp
from jax import lax
from jax.experimental import pallas as pl
from jax.experimental.pallas import tpu as pltpu
from jax.sharding import PartitionSpec as P

score_scale = 192.0 ** (-0.5)
route_scale = 2.5
far_below = -1e30
MIB = 1 << 20
F32 = jnp.float32
BF16 = jnp.bfloat16


def flip(index, mask, size):
    out, bit = 0, 1
    while bit < size:
        here = index // bit % 2
        out = out + bit * ((here + 1) % 2 if mask & bit else here)
        bit *= 2
    return out


def gate_table(owners, per_group, groups, picks, levels):
    rows = picks.shape[1]
    level = levels[...].astype(F32)
    gates = route_scale * level / jnp.sum(level, axis=0, keepdims=True)
    group = groups[...]
    pick = picks[...]
    expert = pick
    for s in range(group.shape[0]):
        inside = (pick >= s * per_group) & (pick < (s + 1) * per_group)
        expert = jnp.where(inside, pick + (group[s : s + 1, :] - s) * per_group, expert)
    same = lax.broadcasted_iota(jnp.int32, (rows, rows), 0) == lax.broadcasted_iota(jnp.int32, (rows, rows), 1)
    lane = lax.broadcasted_iota(jnp.int32, (rows, 128), 1)
    total = jnp.zeros((rows, 128), F32)
    for e in range(owners):
        along = jnp.sum(jnp.where(expert == e, gates, 0.0), axis=0, keepdims=True)
        down = jnp.sum(jnp.where(same, along, 0.0), axis=1, keepdims=True)
        total += jnp.where(lane == e, down, 0.0)
    return total


def layer_kernel(
    dp, tp, per_group, lengths, resid, groups, picks, levels,
    ql_h, qr_h, cl_h, cr_h, vu_h, wo_h, wg_h, wu_h, wd_h, out,
    ql, qr, cl, cr, vu, mix, wo, wg, wu, wd, rblk, head, hbuf, cbuf, resb, acc, pbuf, rbuf, hid,
    accg, accu, pd, sr, xr, zs, zr, fin, hcat,
    l_sem, r_sem, w_sem, c_s, c_r, a_s, a_r, f_s, f_r, q_s, q_r, b_s, b_r, z_s, z_r, x_s, x_r, y_s, y_r,
    d_s, d_r, e_s, e_r, g_s, g_r, o_s, o_r,
):
    d = lax.axis_index("dp")
    t = lax.axis_index("tensor")
    chips = dp // 2
    chip, core = d // 2, d % 2
    sib = chip * 2 + (1 - core)
    row_n = resid.shape[0]
    rows = dp * row_n
    quarter = rows // tp
    depth, cols = wo.shape
    per_quarter = dp // tp
    cpq = chips // tp
    near_first = list(range(1, chips))
    far_first = near_first[::-1]
    steps = row_n // cl.shape[1]
    step_rows = cl.shape[1]
    heads, positions = ql.shape[1], cl.shape[2]
    width = vu.shape[2]

    def send(src, dst, ss, rs, **where):
        return pltpu.make_async_remote_copy(
            src_ref=src, dst_ref=dst, send_sem=ss, recv_sem=rs,
            device_id=where, device_id_type=pl.DeviceIdType.MESH,
        )

    def over(mask):
        return flip(chip, mask, chips) * 2 + core

    barrier = pltpu.get_barrier_semaphore()
    for k in range(1, dp):
        pl.semaphore_signal(barrier, inc=1, device_id={"dp": (d + k) % dp}, device_id_type=pl.DeviceIdType.MESH)
    for k in range(1, tp):
        pl.semaphore_signal(barrier, inc=1, device_id={"tensor": (t + k) % tp}, device_id_type=pl.DeviceIdType.MESH)

    def fetch(step, slot):
        at = pl.ds(step * step_rows, step_rows)
        return (
            pltpu.make_async_copy(cl_h.at[at], cl.at[slot], l_sem.at[slot]),
            pltpu.make_async_copy(cr_h.at[at], cr.at[slot], r_sem.at[slot]),
        )

    loads = [
        pltpu.make_async_copy(src, dst, w_sem.at[i])
        for i, (src, dst) in enumerate((
            (wo_h, wo), (wg_h.at[0], wg), (wu_h.at[0], wu), (wd_h.at[0], wd), (vu_h, vu), (ql_h, ql), (qr_h, qr),
        ))
    ]
    loads[5].start()
    loads[6].start()
    for copy in fetch(0, 0):
        copy.start()
    for j in range(dp):
        rblk[j] = resid[:, j * cols : (j + 1) * cols]
    cbuf[d] = gate_table(dp, per_group, groups, picks, levels)
    loads[5].wait()
    loads[6].wait()

    @pl.loop(0, steps)
    def _attend(step):
        slot = step % 2

        @pl.when(step + 1 < steps)
        def _next():
            for copy in fetch(step + 1, 1 - slot):
                copy.start()

        @pl.when(step == 0)
        def _later():
            loads[4].start()
            loads[0].start()

        @pl.when(step == 1)
        def _latest():
            for i in (1, 2, 3):
                loads[i].start()

        for copy in fetch(step, slot):
            copy.wait()
        place = lax.broadcasted_iota(jnp.int32, (heads, positions), 1)
        base = step * step_rows
        span = range(step_rows)
        scores = [
            lax.dot_general(ql[base + i], cl[slot, i], (((1,), (1,)), ((), ())), preferred_element_type=F32)
            + jnp.dot(qr[base + i], cr[slot, i], preferred_element_type=F32)
            for i in span
        ]
        scores = [jnp.where(place < lengths[base + i], scores[i] * score_scale, far_below) for i in span]
        highest = [jnp.max(scores[i], axis=1, keepdims=True) for i in span]
        raised = [jnp.exp(scores[i] - highest[i]) for i in span]
        totals = [jnp.sum(raised[i], axis=1, keepdims=True) for i in span]
        for i in span:
            mix[base + i] = jnp.dot(raised[i].astype(BF16), cl[slot, i], preferred_element_type=F32) / totals[i]

    pl.semaphore_wait(barrier, dp - 1 + tp - 1)
    pending = []

    coefs = []
    for k in range(1, dp):
        coefs.append(send(cbuf.at[d], cbuf.at[d], c_s.at[k], c_r.at[k], dp=(d + k) % dp))
        coefs[-1].start()
    pending += coefs

    mine = d // per_quarter == t
    slot = d % per_quarter
    shares = [
        send(rblk.at[(d + k) % dp], resb.at[slot], q_s.at[k], q_r.at[slot], dp=(d + k) % dp)
        for k in range(1, dp)
    ]

    @pl.when(mine)
    def _share():
        for copy in shares:
            copy.start()
        resb[slot] = rblk[d]

    loads[4].wait()
    for h in range(heads):
        mixed = mix[:, h, :].astype(BF16)
        value = jnp.dot(mixed, vu[h], preferred_element_type=F32)
        head[:, h * width : (h + 1) * width] = value.astype(BF16)

    gather = {0: send(head, hbuf.at[d], a_s.at[0], a_r.at[0], dp=sib)}
    for j in near_first:
        gather[j] = send(head, hbuf.at[d], a_s.at[j], a_r.at[j], dp=over(j))
    for j in near_first + [0]:
        gather[j].start()
    pending += gather.values()
    hbuf[d] = head[...]
    loads[0].wait()

    forwards = {}

    def pass_on(m):
        for j in range(m * cpq, (m + 1) * cpq):
            if j:
                gather[j].wait_recv()
                block = over(j)
                forwards[j] = send(hbuf.at[block], hbuf.at[block], f_s.at[j], f_r.at[j], dp=sib)
                forwards[j].start()

    chunk = 1024
    sums = []
    pass_on(0)
    for m in range(tp):
        for j in range(m * cpq, (m + 1) * cpq):
            (forwards[j] if j else gather[0]).wait_recv()
        if m >= 1 and m + 1 < tp:
            pass_on(m + 1)
        which = flip(chip // cpq, m, tp)
        blocks = pl.ds(which * per_quarter, per_quarter)
        acc[which] = jnp.zeros((quarter, cols), F32)

        @pl.loop(0, depth // chunk)
        def _project(k):
            at = pl.ds(pl.multiple_of(k * chunk, chunk), chunk)
            acc[which] += jnp.dot(
                hbuf[blocks, :, at].reshape(quarter, chunk), wo[at, :], preferred_element_type=F32
            )

        if m == 0 and tp > 1:
            pass_on(1)
        pbuf[which] = acc[which].astype(BF16)
        place = (which - t + tp) % tp

        @pl.when(which != t)
        def _sum():
            send(pbuf.at[which], rbuf.at[place], b_s.at[m], b_r.at[place], tensor=which).start()

        sums.append((which, place))
    pending += forwards.values()
    for i in range(per_quarter):
        owner = t * per_quarter + i

        @pl.when(owner != d)
        def _arrive():
            send(rblk.at[0], resb.at[i], q_s.at[0], q_r.at[i], dp=owner).wait_recv()

    my_rows = pl.ds(pl.multiple_of(t * quarter, quarter), quarter)
    piece = acc[t]
    for k in range(1, tp):
        send(pbuf.at[0], rbuf.at[k], b_s.at[0], b_r.at[k], tensor=(t + k) % tp).wait_recv()
        piece += rbuf[k].astype(F32)
    attention = piece.astype(BF16).astype(F32)
    hid[d, my_rows, :] = (attention + resb[...].reshape(quarter, cols).astype(F32)).astype(BF16)

    along = []
    for k in range(1, tp):
        along.append(send(hid.at[d, my_rows], hid.at[d, my_rows], z_s.at[k], z_r.at[k], tensor=(t + k) % tp))
        along[-1].start()
    pending += along
    spread = {}
    for k in range(tp):
        if k:
            along[k - 1].wait_recv()
        at = pl.ds(pl.multiple_of((t + tp - k) % tp * quarter, quarter), quarter)
        for j in near_first:
            spread[k, j] = send(hid.at[d, at], hid.at[d, at], x_s.at[k, j], x_r.at[k, j], dp=over(j))
            spread[k, j].start()
        spread[k, 0] = send(hid.at[d, at], hid.at[d, at], x_s.at[k, 0], x_r.at[k, 0], dp=sib)
        spread[k, 0].start()
    pending += spread.values()

    loads[1].wait()
    loads[2].wait()
    accg[...] = jnp.zeros_like(accg)
    accu[...] = jnp.zeros_like(accu)

    def expand(block):
        at = pl.ds(pl.multiple_of(block * cols, cols), cols)
        values = hid[block]
        accg[...] += jnp.dot(values, wg[at, :], preferred_element_type=F32)
        accu[...] += jnp.dot(values, wu[at, :], preferred_element_type=F32)

    expand(d)
    passed = {}
    for k in range(tp):
        at = pl.ds(pl.multiple_of((t + tp - k) % tp * quarter, quarter), quarter)
        for j in near_first:
            spread[k, j].wait_recv()
            block = over(j)
            passed[k, j] = send(hid.at[block, at], hid.at[block, at], y_s.at[k, j], y_r.at[k, j], dp=sib)
            passed[k, j].start()
    pending += passed.values()
    for k in range(tp):
        spread[k, 0].wait_recv()

    @pl.loop(0, chips - 1)
    def _same(j):
        expand((chip + 1 + j) % chips * 2 + core)

    expand(sib)
    for copy in passed.values():
        copy.wait_recv()

    @pl.loop(0, chips - 1)
    def _other(j):
        expand((chip + 1 + j) % chips * 2 + 1 - core)

    for copy in coefs:
        copy.wait_recv()
    table = cbuf[...].reshape(rows, 128)
    lane = lax.broadcasted_iota(jnp.int32, (rows, 128), 1)
    weight = jnp.sum(jnp.where(lane == d, table, 0.0), axis=1, keepdims=True)
    gated = accg[...]
    active = (gated / (1.0 + jnp.exp(-gated)) * accu[...] * weight).astype(BF16)

    loads[3].wait()
    split, part = fin.shape[1], fin.shape[3]
    pieces = [(s, k) for s in range(split) for k in list(range(1, tp)) + [0]]
    halves = []
    for n, (s, k) in enumerate(pieces):
        at = pl.ds(pl.multiple_of(((t + k) % tp * split + s) * part, part), part)
        produced = jnp.dot(active, wd[:, at], preferred_element_type=F32).astype(BF16)
        for b in range(dp):
            pd[n, b % 2, b // 2] = produced[b * row_n : (b + 1) * row_n, :]
        halves.append(send(pd.at[n, 1 - core], sr.at[n], d_s.at[n], d_r.at[n], dp=sib))
        halves[-1].start()
    pending += halves
    across = {}
    for n in range(len(pieces)):
        halves[n].wait_recv()
        pd[n, core] = (pd[n, core].astype(F32) + sr[n].astype(F32)).astype(BF16)
        for j in far_first:
            peer = flip(chip, j, chips)
            across[n, j] = send(pd.at[n, core, peer], xr.at[n, j - 1], e_s.at[n, j], e_r.at[n, j], dp=peer * 2 + core)
            across[n, j].start()
    pending += across.values()
    own_rows = pl.ds(pl.multiple_of(d * row_n, row_n), row_n)
    reduced = {}
    last = []
    for n, (s, k) in enumerate(pieces):
        total = pd[n, core, chip].astype(F32)
        for j in far_first:
            across[n, j].wait_recv()
            total += xr[n, j - 1].astype(F32)
        if k:
            zs[n] = total.astype(BF16)
            reduced[s, k] = send(zs.at[n], zr.at[n], g_s.at[n], g_r.at[n], tensor=(t + k) % tp)
            reduced[s, k].start()
        else:
            first = (t * split + s) * part // cols
            for i in range(part // cols):
                hcat[:, i * cols : (i + 1) * cols] = hid[first + i, own_rows, :].astype(F32)
            for m in range(1, tp):
                reduced[s, m].wait_recv()
                total += zr[s * tp + m - 1].astype(F32)
            fin[t, s] = (hcat[...] + total).astype(BF16)
            for m in range(1, tp):
                last.append(send(fin.at[t, s], fin.at[t, s], o_s.at[s, m], o_r.at[s, m], tensor=(t + m) % tp))
                last[-1].start()
    pending += reduced.values()
    pending += last
    for copy in last:
        copy.wait_recv()
    for c in range(tp):
        for s in range(split):
            out[:, (c * split + s) * part : (c * split + s + 1) * part] = fin[c, s]
    for copy in pending:
        copy.wait_send()
    for m, (which, place) in enumerate(sums):

        @pl.when(which != t)
        def _summed():
            send(pbuf.at[which], rbuf.at[place], b_s.at[m], b_r.at[place], tensor=which).wait_send()

    @pl.when(mine)
    def _shared():
        for copy in shares:
            copy.wait_send()


def local(
    dp, tp, residual, query_latent, query_rope, cache_latent, cache_rope, lengths, value_up, out_proj,
    gate_proj, up_proj, down_proj, groups, expert_picks, gate_levels,
):
    row_n, model = residual.shape
    per_group = dp // min(8, dp // 2)
    rows = dp * row_n
    depth, cols = out_proj.shape
    units = gate_proj.shape[2]
    heads, lat = query_latent.shape[1:]
    quarter = rows // tp
    split = 2
    part = model // (tp * split)
    count = tp * split
    chips = dp // 2
    step_rows = 4
    vm = lambda *shape: pltpu.VMEM(shape, BF16)
    wide = lambda *shape: pltpu.VMEM(shape, F32)
    sem = lambda *shape: pltpu.SemaphoreType.DMA(shape)
    return pl.pallas_call(
        functools.partial(layer_kernel, dp, tp, per_group),
        out_shape=jax.ShapeDtypeStruct((row_n, model), BF16),
        in_specs=[pl.BlockSpec(memory_space=pltpu.SMEM)]
        + [pl.BlockSpec(memory_space=pltpu.VMEM)] * 4
        + [pl.BlockSpec(memory_space=pl.ANY)] * 9,
        out_specs=pl.BlockSpec(memory_space=pltpu.VMEM),
        scratch_shapes=[
            vm(*query_latent.shape), vm(*query_rope.shape),
            vm(2, step_rows, *cache_latent.shape[1:]), vm(2, step_rows, *cache_rope.shape[1:]),
            vm(*value_up.shape), wide(row_n, heads, lat),
            vm(depth, cols), vm(model, units), vm(model, units), vm(units, model),
            vm(dp, row_n, cols), vm(row_n, depth), vm(dp, row_n, depth), wide(dp, row_n, 128),
            vm(dp // tp, row_n, cols),
            wide(tp, quarter, cols), vm(tp, quarter, cols), vm(tp, quarter, cols),
            vm(dp, rows, cols), wide(rows, units), wide(rows, units),
            vm(count, 2, chips, row_n, part), vm(count, chips, row_n, part),
            vm(count, chips - 1, row_n, part), vm(count, row_n, part), vm(count, row_n, part),
            vm(tp, split, row_n, part), wide(row_n, part),
            sem(2), sem(2), sem(7), sem(dp), sem(dp), sem(chips), sem(chips), sem(chips), sem(chips),
            sem(dp), sem(dp // tp), sem(tp), sem(tp), sem(tp), sem(tp),
            sem(tp, chips), sem(tp, chips), sem(tp, chips), sem(tp, chips),
            sem(count), sem(count), sem(count, chips), sem(count, chips), sem(count), sem(count),
            sem(split, tp), sem(split, tp),
        ],
        compiler_params=pltpu.CompilerParams(
            collective_id=0, has_side_effects=True, vmem_limit_bytes=60 * MIB
        ),
        cost_estimate=pl.CostEstimate(
            flops=2 * rows * (depth * cols + 3 * model * units) + 2 * row_n * heads * 1024 * 1088,
            bytes_accessed=42 * MIB, transcendentals=0,
        ),
    )(
        lengths, residual, groups.T, expert_picks.T, gate_levels.T, query_latent, query_rope,
        cache_latent, cache_rope, value_up, out_proj, gate_proj, up_proj, down_proj,
    )


def solution(mesh):
    return jax.shard_map(
        functools.partial(local, mesh.shape["dp"], mesh.shape["tensor"]),
        mesh=mesh,
        in_specs=(
            P("dp", None),
            P("dp", "tensor", None),
            P("dp", "tensor", None),
            P("dp", None, None),
            P("dp", None, None),
            P("dp"),
            P("tensor", None, None),
            P("tensor", "dp"),
            P("dp", None, "tensor"),
            P("dp", None, "tensor"),
            P("dp", "tensor", None),
            P("dp", None),
            P("dp", None),
            P("dp", None),
        ),
        out_specs=P("dp", None),
        check_vma=False,
    )
```

time: 94.7 us -> 81.8 us (0.86)
  local copies, waits for them, and re-layouts: 11.6 us -> 1.64 us
  other arithmetic: 2.67 us -> 0 us
    unnamed x21 -> x1, local copies, waits for them, and re-layouts: 11.5 us -> 1.64 us
    unnamed x2 -> x0, other arithmetic: 1.94 us -> none
    pallas_call x2 -> x1, Pallas kernels: 80 us -> 80 us  [local(): pl.pallas_call(functools.partial(layer_kernel, dp, tp, per_group), out_sh...]
where the time goes in v2:
time: 81.8 us; the launch traced here: 81.7 us
  Pallas kernels  80 us (98%)
  local copies, waits for them, and re-layouts  1.64 us (2%)
    pallas_call x1, Pallas kernels, local(): pl.pallas_call(functools.partial(layer_kernel, dp, tp, per_group), out_sh...  80 us
    unnamed x1, local copies, waits for them, and re-layouts  1.64 us

profile of v2, /device:TPU:0, one launch (start us, length us, event | category | flops | bytes accessed | tf_op | source)
XLA Modules:
  0.0 81.7 jit_solution(10548315184944954989)
XLA Ops:
  0.0 80.0 %shard_map.136 = bf16[16,7168]{1,0:T(8,128)(2,1)} custom-call(s32[16]{0:T(128)} %lengths.1, bf16[16,7168]{1,0:T(8,128)(2,1)} %resid.1, s32[4,16]{1,0:T(4,128)} %bitcast.5, s32[8,16]{1,0:T(8,128)} %bitcast.3, s32[8,16]{1,0:T(8,128)} %bitcast.4, bf16[16,32,512]{2,1,0:T(8,128)(2,1)} %ql_h.1, bf16[16,32,64]{2,1,0:T(8,128)(2,1)} %qr_h.1, ...), custom_call_target="tpu_custom_call" | custom-call | flops 3489660928 | bytes 44040192 | tf_op jit(solution)/shard_map/pallas_call | solution.py:384
  80.0 1.6 %copy.16 = bf16[16,7168]{1,0:T(8,128)(2,1)} copy(bf16[16,7168]{1,0:T(8,128)(2,1)} %shard_map.136) | data formatting | bytes 458752

commit v3 on v2

--- a/solution.py
+++ b/solution.py
@@ -46,9 +46,9 @@
 
 def layer_kernel(
     dp, tp, per_group, lengths, resid, groups, picks, levels,
-    ql_h, qr_h, cl_h, cr_h, vu_h, wo_h, wg_h, wu_h, wd_h, out,
-    ql, qr, cl, cr, vu, mix, wo, wg, wu, wd, rblk, head, hbuf, cbuf, resb, acc, pbuf, rbuf, hid,
-    accg, accu, pd, sr, xr, zs, zr, fin, hcat,
+    ql_h, qr_h, cl_h, cr_h, vu_h, wo_h, wg_h, wu_h, wd_h, hid_out, out,
+    ql, qr, cl, cr, vu, mix, wo, wg, wu, wd, rblk, hbuf, cbuf, resb, acc, pbuf, rbuf, hid,
+    accg, accu, pd, sr, xr, zs, zr, fin,
     l_sem, r_sem, w_sem, c_s, c_r, a_s, a_r, f_s, f_r, q_s, q_r, b_s, b_r, z_s, z_r, x_s, x_r, y_s, y_r,
     d_s, d_r, e_s, e_r, g_s, g_r, o_s, o_r,
 ):
@@ -62,13 +62,15 @@
     quarter = rows // tp
     depth, cols = wo.shape
     per_quarter = dp // tp
-    cpq = chips // tp
     near_first = list(range(1, chips))
     far_first = near_first[::-1]
     steps = row_n // cl.shape[1]
     step_rows = cl.shape[1]
     heads, positions = ql.shape[1], cl.shape[2]
     width = vu.shape[2]
+    rope = qr.shape[2]
+    parts = hbuf.shape[0]
+    chunk = depth // parts
 
     def send(src, dst, ss, rs, **where):
         return pltpu.make_async_remote_copy(
@@ -132,9 +134,16 @@
         place = lax.broadcasted_iota(jnp.int32, (heads, positions), 1)
         base = step * step_rows
         span = range(step_rows)
+        ropes = qr[pl.ds(base, step_rows)].reshape(step_rows * heads, rope)
+        spread_q = jnp.concatenate([ropes] * step_rows, axis=1)
+        from_row = lax.broadcasted_iota(jnp.int32, spread_q.shape, 0) // heads
+        to_row = lax.broadcasted_iota(jnp.int32, spread_q.shape, 1) // rope
+        spread_q = jnp.where(from_row == to_row, spread_q.astype(F32), 0.0).astype(BF16)
+        keys = cr[slot].reshape(step_rows * rope, positions)
+        rope_scores = jnp.dot(spread_q, keys, preferred_element_type=F32)
         scores = [
             lax.dot_general(ql[base + i], cl[slot, i], (((1,), (1,)), ((), ())), preferred_element_type=F32)
-            + jnp.dot(qr[base + i], cr[slot, i], preferred_element_type=F32)
+            + rope_scores[i * heads : (i + 1) * heads, :]
             for i in span
         ]
         scores = [jnp.where(place < lengths[base + i], scores[i] * score_scale, far_below) for i in span]
@@ -167,60 +176,52 @@
         resb[slot] = rblk[d]
 
     loads[4].wait()
-    for h in range(heads):
-        mixed = mix[:, h, :].astype(BF16)
-        value = jnp.dot(mixed, vu[h], preferred_element_type=F32)
-        head[:, h * width : (h + 1) * width] = value.astype(BF16)
-
-    gather = {0: send(head, hbuf.at[d], a_s.at[0], a_r.at[0], dp=sib)}
-    for j in near_first:
-        gather[j] = send(head, hbuf.at[d], a_s.at[j], a_r.at[j], dp=over(j))
-    for j in near_first + [0]:
-        gather[j].start()
+    gather = {}
+    for p in range(parts):
+        for h in range(p * heads // parts, (p + 1) * heads // parts, 2):
+            mixed = jnp.concatenate([mix[:, h, :], mix[:, h + 1, :]], axis=0).astype(BF16)
+            both = jnp.concatenate([vu[h], vu[h + 1]], axis=1)
+            value = jnp.dot(mixed, both, preferred_element_type=F32).astype(BF16)
+            at = h * width - p * chunk
+            hbuf[p, d, :, at : at + width] = value[:row_n, :width]
+            hbuf[p, d, :, at + width : at + 2 * width] = value[row_n:, width:]
+        block = hbuf.at[p, d]
+        for j in near_first + [0]:
+            gather[p, j] = send(block, block, a_s.at[p, j], a_r.at[p, j], dp=over(j) if j else sib)
+            gather[p, j].start()
     pending += gather.values()
-    hbuf[d] = head[...]
     loads[0].wait()
 
     forwards = {}
-
-    def pass_on(m):
-        for j in range(m * cpq, (m + 1) * cpq):
-            if j:
-                gather[j].wait_recv()
-                block = over(j)
-                forwards[j] = send(hbuf.at[block], hbuf.at[block], f_s.at[j], f_r.at[j], dp=sib)
-                forwards[j].start()
-
-    chunk = 1024
+    for p in range(parts):
+        for j in near_first:
+            gather[p, j].wait_recv()
+            block = hbuf.at[p, over(j)]
+            forwards[p, j] = send(block, block, f_s.at[p, j], f_r.at[p, j], dp=sib)
+            forwards[p, j].start()
+        gather[p, 0].wait_recv()
+        for j in near_first:
+            forwards[p, j].wait_recv()
+        fine = min(512, chunk)
+        if p == 0:
+            acc[...] = jnp.zeros_like(acc)
+
+        @pl.loop(0, chunk // fine)
+        def _project(k):
+            at = pl.ds(pl.multiple_of(k * fine, fine), fine)
+            down = pl.ds(pl.multiple_of(p * chunk + k * fine, fine), fine)
+            acc[...] += jnp.dot(
+                hbuf[p, :, :, at].reshape(rows, fine), wo[down, :], preferred_element_type=F32
+            ).reshape(acc.shape)
+
+    pending += forwards.values()
+    pbuf[...] = acc[...].astype(BF16)
     sums = []
-    pass_on(0)
-    for m in range(tp):
-        for j in range(m * cpq, (m + 1) * cpq):
-            (forwards[j] if j else gather[0]).wait_recv()
-        if m >= 1 and m + 1 < tp:
-            pass_on(m + 1)
-        which = flip(chip // cpq, m, tp)
-        blocks = pl.ds(which * per_quarter, per_quarter)
-        acc[which] = jnp.zeros((quarter, cols), F32)
-
-        @pl.loop(0, depth // chunk)
-        def _project(k):
-            at = pl.ds(pl.multiple_of(k * chunk, chunk), chunk)
-            acc[which] += jnp.dot(
-                hbuf[blocks, :, at].reshape(quarter, chunk), wo[at, :], preferred_element_type=F32
-            )
-
-        if m == 0 and tp > 1:
-            pass_on(1)
-        pbuf[which] = acc[which].astype(BF16)
-        place = (which - t + tp) % tp
-
-        @pl.when(which != t)
-        def _sum():
-            send(pbuf.at[which], rbuf.at[place], b_s.at[m], b_r.at[place], tensor=which).start()
-
-        sums.append((which, place))
-    pending += forwards.values()
+    for k in range(1, tp):
+        u = (t + k) % tp
+        sums.append(send(pbuf.at[u], rbuf.at[k], b_s.at[k], b_r.at[k], tensor=u))
+        sums[-1].start()
+    pending += sums
     for i in range(per_quarter):
         owner = t * per_quarter + i
 
@@ -231,7 +232,7 @@
     my_rows = pl.ds(pl.multiple_of(t * quarter, quarter), quarter)
     piece = acc[t]
     for k in range(1, tp):
-        send(pbuf.at[0], rbuf.at[k], b_s.at[0], b_r.at[k], tensor=(t + k) % tp).wait_recv()
+        sums[k - 1].wait_recv()
         piece += rbuf[k].astype(F32)
     attention = piece.astype(BF16).astype(F32)
     hid[d, my_rows, :] = (attention + resb[...].reshape(quarter, cols).astype(F32)).astype(BF16)
@@ -267,6 +268,10 @@
     expand(d)
     passed = {}
     for k in range(tp):
+        if k == tp - 1:
+            for m in range(tp):
+                spread[m, 0].wait_recv()
+            expand(sib)
         at = pl.ds(pl.multiple_of((t + tp - k) % tp * quarter, quarter), quarter)
         for j in near_first:
             spread[k, j].wait_recv()
@@ -274,14 +279,11 @@
             passed[k, j] = send(hid.at[block, at], hid.at[block, at], y_s.at[k, j], y_r.at[k, j], dp=sib)
             passed[k, j].start()
     pending += passed.values()
-    for k in range(tp):
-        spread[k, 0].wait_recv()
 
     @pl.loop(0, chips - 1)
     def _same(j):
         expand((chip + 1 + j) % chips * 2 + core)
 
-    expand(sib)
     for copy in passed.values():
         copy.wait_recv()
 
@@ -301,6 +303,16 @@
     split, part = fin.shape[1], fin.shape[3]
     pieces = [(s, k) for s in range(split) for k in list(range(1, tp)) + [0]]
     halves = []
+    across = {}
+
+    def cross(n):
+        halves[n].wait_recv()
+        pd[n, core] = (pd[n, core].astype(F32) + sr[n].astype(F32)).astype(BF16)
+        for j in far_first:
+            peer = flip(chip, j, chips)
+            across[n, j] = send(pd.at[n, core, peer], xr.at[n, j - 1], e_s.at[n, j], e_r.at[n, j], dp=peer * 2 + core)
+            across[n, j].start()
+
     for n, (s, k) in enumerate(pieces):
         at = pl.ds(pl.multiple_of(((t + k) % tp * split + s) * part, part), part)
         produced = jnp.dot(active, wd[:, at], preferred_element_type=F32).astype(BF16)
@@ -308,17 +320,15 @@
             pd[n, b % 2, b // 2] = produced[b * row_n : (b + 1) * row_n, :]
         halves.append(send(pd.at[n, 1 - core], sr.at[n], d_s.at[n], d_r.at[n], dp=sib))
         halves[-1].start()
+        if n >= 2:
+            cross(n - 2)
+    cross(len(pieces) - 2)
+    cross(len(pieces) - 1)
     pending += halves
-    across = {}
-    for n in range(len(pieces)):
-        halves[n].wait_recv()
-        pd[n, core] = (pd[n, core].astype(F32) + sr[n].astype(F32)).astype(BF16)
-        for j in far_first:
-            peer = flip(chip, j, chips)
-            across[n, j] = send(pd.at[n, core, peer], xr.at[n, j - 1], e_s.at[n, j], e_r.at[n, j], dp=peer * 2 + core)
-            across[n, j].start()
     pending += across.values()
     own_rows = pl.ds(pl.multiple_of(d * row_n, row_n), row_n)
+    for b in range(dp):
+        hid_out[:, b * cols : (b + 1) * cols] = hid[b, own_rows, :]
     reduced = {}
     last = []
     for n, (s, k) in enumerate(pieces):
@@ -331,13 +341,10 @@
             reduced[s, k] = send(zs.at[n], zr.at[n], g_s.at[n], g_r.at[n], tensor=(t + k) % tp)
             reduced[s, k].start()
         else:
-            first = (t * split + s) * part // cols
-            for i in range(part // cols):
-                hcat[:, i * cols : (i + 1) * cols] = hid[first + i, own_rows, :].astype(F32)
             for m in range(1, tp):
                 reduced[s, m].wait_recv()
                 total += zr[s * tp + m - 1].astype(F32)
-            fin[t, s] = (hcat[...] + total).astype(BF16)
+            fin[t, s] = total.astype(BF16)
             for m in range(1, tp):
                 last.append(send(fin.at[t, s], fin.at[t, s], o_s.at[s, m], o_r.at[s, m], tensor=(t + m) % tp))
                 last[-1].start()
@@ -350,11 +357,6 @@
             out[:, (c * split + s) * part : (c * split + s + 1) * part] = fin[c, s]
     for copy in pending:
         copy.wait_send()
-    for m, (which, place) in enumerate(sums):
-
-        @pl.when(which != t)
-        def _summed():
-            send(pbuf.at[which], rbuf.at[place], b_s.at[m], b_r.at[place], tensor=which).wait_send()
 
     @pl.when(mine)
     def _shared():
@@ -381,26 +383,26 @@
     vm = lambda *shape: pltpu.VMEM(shape, BF16)
     wide = lambda *shape: pltpu.VMEM(shape, F32)
     sem = lambda *shape: pltpu.SemaphoreType.DMA(shape)
-    return pl.pallas_call(
+    hidden, routed = pl.pallas_call(
         functools.partial(layer_kernel, dp, tp, per_group),
-        out_shape=jax.ShapeDtypeStruct((row_n, model), BF16),
+        out_shape=[jax.ShapeDtypeStruct((row_n, model), BF16)] * 2,
         in_specs=[pl.BlockSpec(memory_space=pltpu.SMEM)]
         + [pl.BlockSpec(memory_space=pltpu.VMEM)] * 4
         + [pl.BlockSpec(memory_space=pl.ANY)] * 9,
-        out_specs=pl.BlockSpec(memory_space=pltpu.VMEM),
+        out_specs=[pl.BlockSpec(memory_space=pltpu.VMEM)] * 2,
         scratch_shapes=[
             vm(*query_latent.shape), vm(*query_rope.shape),
             vm(2, step_rows, *cache_latent.shape[1:]), vm(2, step_rows, *cache_rope.shape[1:]),
             vm(*value_up.shape), wide(row_n, heads, lat),
             vm(depth, cols), vm(model, units), vm(model, units), vm(units, model),
-            vm(dp, row_n, cols), vm(row_n, depth), vm(dp, row_n, depth), wide(dp, row_n, 128),
+            vm(dp, row_n, cols), vm(2, dp, row_n, depth // 2), wide(dp, row_n, 128),
             vm(dp // tp, row_n, cols),
             wide(tp, quarter, cols), vm(tp, quarter, cols), vm(tp, quarter, cols),
             vm(dp, rows, cols), wide(rows, units), wide(rows, units),
             vm(count, 2, chips, row_n, part), vm(count, chips, row_n, part),
             vm(count, chips - 1, row_n, part), vm(count, row_n, part), vm(count, row_n, part),
-            vm(tp, split, row_n, part), wide(row_n, part),
-            sem(2), sem(2), sem(7), sem(dp), sem(dp), sem(chips), sem(chips), sem(chips), sem(chips),
+            vm(tp, split, row_n, part),
+            sem(2), sem(2), sem(7), sem(dp), sem(dp), sem(2, chips), sem(2, chips), sem(2, chips), sem(2, chips),
             sem(dp), sem(dp // tp), sem(tp), sem(tp), sem(tp), sem(tp),
             sem(tp, chips), sem(tp, chips), sem(tp, chips), sem(tp, chips),
             sem(count), sem(count), sem(count, chips), sem(count, chips), sem(count), sem(count),
@@ -417,6 +419,7 @@
         lengths, residual, groups.T, expert_picks.T, gate_levels.T, query_latent, query_rope,
         cache_latent, cache_rope, value_up, out_proj, gate_proj, up_proj, down_proj,
     )
+    return (hidden.astype(F32) + routed.astype(F32)).astype(BF16)
 
 
 def solution(mesh):

time: 81.8 us -> 80.5 us (0.984)
  other arithmetic: 0 us -> 1.79 us
  local copies, waits for them, and re-layouts: 1.64 us -> 0 us
  Pallas kernels: 80 us -> 78.5 us
    convert_element_type x0 -> x1, other arithmetic: none -> 1.79 us  [local(): return (hidden.astype(F32) + routed.astype(F32)).astype(BF16)]
    unnamed x1 -> x0, local copies, waits for them, and re-layouts: 1.64 us -> none
    pallas_call x1, Pallas kernels: 80 us -> 78.5 us  [local(): pl.pallas_call(functools.partial(layer_kernel, dp, tp, per_group), out_sh...]
where the time goes in v3:
time: 80.5 us; the launch traced here: 80.3 us
  Pallas kernels  78.5 us (98%)
  other arithmetic  1.79 us (2%)
    pallas_call x1, Pallas kernels, local(): pl.pallas_call(functools.partial(layer_kernel, dp, tp, per_group), out_sh...  78.5 us
    convert_element_type x1, other arithmetic, local(): return (hidden.astype(F32) + routed.astype(F32)).astype(BF16)  1.79 us

profile of v3, /device:TPU:0, one launch (start us, length us, event | category | flops | bytes accessed | tf_op | source)
XLA Modules:
  0.0 80.3 jit_solution(15524741099606674239)
XLA Ops:
  0.0 78.5 %shard_map.136 = (bf16[16,7168]{1,0:T(8,128)(2,1)}, bf16[16,7168]{1,0:T(8,128)(2,1)}) custom-call(s32[16]{0:T(128)} %lengths.1, bf16[16,7168]{1,0:T(8,128)(2,1)} %resid.1, s32[4,16]{1,0:T(4,128)} %bitcast.5, s32[8,16]{1,0:T(8,128)} %bitcast.3, s32[8,16]{1,0:T(8,128)} %bitcast.4, bf16[16,32,512]{2,1,0:T(8,128)(2,1)} %ql_h.1, bf16[16,32,64]{2,1,0:T(8,128)(2,1)} %qr_h.1, ...), custom_call_target="tpu_custom_call" | custom-call | flops 3489660928 | bytes 44040192 | tf_op jit(solution)/shard_map/pallas_call | solution.py:386
  78.5 1.8 %add_convert_fusion = bf16[16,7168]{1,0:T(8,128)(2,1)} fusion(bf16[16,7168]{1,0:T(8,128)(2,1)} %get-tuple-element.8, bf16[16,7168]{1,0:T(8,128)(2,1)} %get-tuple-element.7), kind=kLoop, calls=%fused_computation | loop fusion | flops 458752 | bytes 688128 | tf_op jit(solution)/shard_map/convert_element_type | solution.py:422

commit v4 on v3

--- a/solution.py
+++ b/solution.py
@@ -68,7 +68,7 @@
     step_rows = cl.shape[1]
     heads, positions = ql.shape[1], cl.shape[2]
     width = vu.shape[2]
-    rope = qr.shape[2]
+    lat, rope = ql.shape[2], qr.shape[2]
     parts = hbuf.shape[0]
     chunk = depth // parts
 
@@ -131,27 +131,34 @@
 
         for copy in fetch(step, slot):
             copy.wait()
-        place = lax.broadcasted_iota(jnp.int32, (heads, positions), 1)
         base = step * step_rows
-        span = range(step_rows)
-        ropes = qr[pl.ds(base, step_rows)].reshape(step_rows * heads, rope)
-        spread_q = jnp.concatenate([ropes] * step_rows, axis=1)
-        from_row = lax.broadcasted_iota(jnp.int32, spread_q.shape, 0) // heads
-        to_row = lax.broadcasted_iota(jnp.int32, spread_q.shape, 1) // rope
-        spread_q = jnp.where(from_row == to_row, spread_q.astype(F32), 0.0).astype(BF16)
+        lanes = step_rows * heads
+
+        def diagonal(queries, times):
+            tiled = jnp.concatenate([queries] * times, axis=1)
+            from_row = lax.broadcasted_iota(jnp.int32, tiled.shape, 0) // heads
+            to_row = lax.broadcasted_iota(jnp.int32, tiled.shape, 1) // queries.shape[1]
+            return jnp.where(from_row == to_row, tiled.astype(F32), 0.0).astype(BF16)
+
+        latents = jnp.concatenate([cl[slot, i] for i in range(step_rows)], axis=1)
+        q_lat = diagonal(ql[pl.ds(base, step_rows)].reshape(lanes, lat), step_rows)
+        q_rope = diagonal(qr[pl.ds(base, step_rows)].reshape(lanes, rope), step_rows)
         keys = cr[slot].reshape(step_rows * rope, positions)
-        rope_scores = jnp.dot(spread_q, keys, preferred_element_type=F32)
-        scores = [
-            lax.dot_general(ql[base + i], cl[slot, i], (((1,), (1,)), ((), ())), preferred_element_type=F32)
-            + rope_scores[i * heads : (i + 1) * heads, :]
-            for i in span
-        ]
-        scores = [jnp.where(place < lengths[base + i], scores[i] * score_scale, far_below) for i in span]
-        highest = [jnp.max(scores[i], axis=1, keepdims=True) for i in span]
-        raised = [jnp.exp(scores[i] - highest[i]) for i in span]
-        totals = [jnp.sum(raised[i], axis=1, keepdims=True) for i in span]
-        for i in span:
-            mix[base + i] = jnp.dot(raised[i].astype(BF16), cl[slot, i], preferred_element_type=F32) / totals[i]
+        scores = lax.dot_general(latents, q_lat, (((1,), (1,)), ((), ())), preferred_element_type=F32)
+        scores += lax.dot_general(keys, q_rope, (((0,), (1,)), ((), ())), preferred_element_type=F32)
+        lane_row = lax.broadcasted_iota(jnp.int32, (1, lanes), 1) // heads
+        limit = jnp.zeros((1, lanes), jnp.int32)
+        for i in range(step_rows):
+            limit = jnp.where(lane_row == i, lengths[base + i], limit)
+        place = lax.broadcasted_iota(jnp.int32, (positions, lanes), 0)
+        scores = jnp.where(place < limit, scores * score_scale, far_below)
+        raised = jnp.exp(scores - jnp.max(scores, axis=0, keepdims=True))
+        weights = raised * (1.0 / jnp.sum(raised, axis=0, keepdims=True))
+        weights = jnp.transpose(weights).astype(BF16)
+        for i in range(step_rows):
+            mix[base + i] = jnp.dot(
+                weights[i * heads : (i + 1) * heads, :], cl[slot, i], preferred_element_type=F32
+            )
 
     pl.semaphore_wait(barrier, dp - 1 + tp - 1)
     pending = []

time: 80.5 us -> 82.6 us (1.026)
  Pallas kernels: 78.5 us -> 80.6 us
    pallas_call x1, Pallas kernels: 78.5 us -> 80.6 us  [local(): pl.pallas_call(functools.partial(layer_kernel, dp, tp, per_group), out_sh...]
where the time goes in v4:
time: 82.6 us; the launch traced here: 82.4 us
  Pallas kernels  80.6 us (98%)
  other arithmetic  1.79 us (2%)
    pallas_call x1, Pallas kernels, local(): pl.pallas_call(functools.partial(layer_kernel, dp, tp, per_group), out_sh...  80.6 us
    convert_element_type x1, other arithmetic, local(): return (hidden.astype(F32) + routed.astype(F32)).astype(BF16)  1.79 us

profile of v4, /device:TPU:0, one launch (start us, length us, event | category | flops | bytes accessed | tf_op | source)
XLA Modules:
  0.0 82.4 jit_solution(2478215348811667913)
XLA Ops:
  0.0 80.6 %shard_map.136 = (bf16[16,7168]{1,0:T(8,128)(2,1)}, bf16[16,7168]{1,0:T(8,128)(2,1)}) custom-call(s32[16]{0:T(128)} %lengths.1, bf16[16,7168]{1,0:T(8,128)(2,1)} %resid.1, s32[4,16]{1,0:T(4,128)} %bitcast.5, s32[8,16]{1,0:T(8,128)} %bitcast.3, s32[8,16]{1,0:T(8,128)} %bitcast.4, bf16[16,32,512]{2,1,0:T(8,128)(2,1)} %ql_h.1, bf16[16,32,64]{2,1,0:T(8,128)(2,1)} %qr_h.1, ...), custom_call_target="tpu_custom_call" | custom-call | flops 3489660928 | bytes 44040192 | tf_op jit(solution)/shard_map/pallas_call | solution.py:393
  80.6 1.8 %add_convert_fusion = bf16[16,7168]{1,0:T(8,128)(2,1)} fusion(bf16[16,7168]{1,0:T(8,128)(2,1)} %get-tuple-element.8, bf16[16,7168]{1,0:T(8,128)(2,1)} %get-tuple-element.7), kind=kLoop, calls=%fused_computation | loop fusion | flops 458752 | bytes 688128 | tf_op jit(solution)/shard_map/convert_element_type | solution.py:429

commit v5 on v3

--- a/solution.py
+++ b/solution.py
@@ -124,11 +124,6 @@
             loads[4].start()
             loads[0].start()
 
-        @pl.when(step == 1)
-        def _latest():
-            for i in (1, 2, 3):
-                loads[i].start()
-
         for copy in fetch(step, slot):
             copy.wait()
         place = lax.broadcasted_iota(jnp.int32, (heads, positions), 1)
@@ -153,6 +148,8 @@
         for i in span:
             mix[base + i] = jnp.dot(raised[i].astype(BF16), cl[slot, i], preferred_element_type=F32) / totals[i]
 
+    for i in (1, 2, 3):
+        loads[i].start()
     pl.semaphore_wait(barrier, dp - 1 + tp - 1)
     pending = []
 

time: 80.5 us -> 78.2 us (0.971)
  Pallas kernels: 78.5 us -> 76.2 us
    pallas_call x1, Pallas kernels: 78.5 us -> 76.2 us  [local(): pl.pallas_call(functools.partial(layer_kernel, dp, tp, per_group), out_sh...]
where the time goes in v5:
time: 78.2 us; the launch traced here: 78 us
  Pallas kernels  76.2 us (97%)
  other arithmetic  1.79 us (2%)
    pallas_call x1, Pallas kernels, local(): pl.pallas_call(functools.partial(layer_kernel, dp, tp, per_group), out_sh...  76.2 us
    convert_element_type x1, other arithmetic, local(): return (hidden.astype(F32) + routed.astype(F32)).astype(BF16)  1.79 us

profile of v5, /device:TPU:0, one launch (start us, length us, event | category | flops | bytes accessed | tf_op | source)
XLA Modules:
  0.0 78.0 jit_solution(1120134537505223710)
XLA Ops:
  0.0 76.2 %shard_map.136 = (bf16[16,7168]{1,0:T(8,128)(2,1)}, bf16[16,7168]{1,0:T(8,128)(2,1)}) custom-call(s32[16]{0:T(128)} %lengths.1, bf16[16,7168]{1,0:T(8,128)(2,1)} %resid.1, s32[4,16]{1,0:T(4,128)} %bitcast.5, s32[8,16]{1,0:T(8,128)} %bitcast.3, s32[8,16]{1,0:T(8,128)} %bitcast.4, bf16[16,32,512]{2,1,0:T(8,128)(2,1)} %ql_h.1, bf16[16,32,64]{2,1,0:T(8,128)(2,1)} %qr_h.1, ...), custom_call_target="tpu_custom_call" | custom-call | flops 3489660928 | bytes 44040192 | tf_op jit(solution)/shard_map/pallas_call | solution.py:383
  76.2 1.8 %add_convert_fusion = bf16[16,7168]{1,0:T(8,128)(2,1)} fusion(bf16[16,7168]{1,0:T(8,128)(2,1)} %get-tuple-element.8, bf16[16,7168]{1,0:T(8,128)(2,1)} %get-tuple-element.7), kind=kLoop, calls=%fused_computation | loop fusion | flops 458752 | bytes 688128 | tf_op jit(solution)/shard_map/convert_element_type | solution.py:419
